TPU v7x, 32 devices: a whole 2x2x4 slice. The times are simulated.
32 devices in a mesh: ocean: 16 (over z, y, core), sht: 2 (over x).
Axes of the slice: x: 2, y: 2, z: 4, core: 2. Of those that a mesh axis runs over, the one named last changes fastest.
Arguments:
- height: float32 [256, 2048], P('ocean', 'sht'), may hold values from -6 to 6
- east: float32 [256, 2048], P('ocean', 'sht'), may hold values from -3 to 3
- north: float32 [256, 2048], P('ocean', 'sht'), may hold values from -3 to 3
- depth: float32 [256, 2048], P('ocean', 'sht'), may hold values from 0.3 to 1.5
- equilibrium: float32 [256, 2048], P('ocean', 'sht'), may hold values from -3 to 3
- mask: int32 [256, 2048], P('ocean', 'sht'), may hold values from 0 to 1, as said below
- sines: float32 [256], P('ocean'), may hold values from -0.95 to 0.95, as said below
- legendre: float32 [256, 1024, 1024], P('ocean', None, 'sht'), as said below
- love: float32 [1024], replicated, may hold values from 0.01 to 0.3
Outputs:
- level_out: float32 [256, 2048], P('ocean', 'sht')
- east_out: float32 [256, 2048], P('ocean', 'sht')
- north_out: float32 [256, 2048], P('ocean', 'sht')
Inputs may be any that keep to these rules, and one draw needn't show every extreme that they name: `mask`: 1 marks ocean, 0 land; rows 0 and 255 and columns 0 and 2047 are land. `sines`: ascending; row j lies within 0.2 / 256 * 1.9 of -0.95 + 1.9 (j + 0.5) / 256. legendre[j, l, m] is the fully normalized associated Legendre function of degree l and order m at sines[j] (unit integral of its square over -1 to 1), zero where l < m.
All inputs are finite; a program needn't handle non-finite values.
Results may differ from a plain program's by a relative error of at most 0.0003.
Values sent between devices are 32-bit elements; how exact they have to be, the bound alone decides.
A program may use at most 128 MiB of HBM per device.

v0:
```python
import math

import jax
import jax.numpy as jnp
from jax import lax
from jax.sharding import PartitionSpec as P

STEPS = 3


COURANT = 0.12
ROTATION = 0.5
FRICTION = 0.3
HIGHEST = lax.Precision.HIGHEST


def extended(x, sides, width):
    for axis, dim in sides:
        peers, length = (lax.axis_size(axis), x.shape[dim])
        up = [(i, (i + 1) % peers) for i in range(peers - 1)]
        down = [(j, i) for i, j in up]
        last = lax.slice_in_dim(x, length - width, length, axis=dim)
        initial = lax.slice_in_dim(x, 0, width, axis=dim)
        before = lax.ppermute(last, axis, up)
        after = lax.ppermute(initial, axis, down)
        x = jnp.concatenate([before, x, after], axis=dim)
    return x


def decode_columns(width, order_dev):
    column = jnp.arange(width, dtype=jnp.int32)
    owner = column // (2 * order_dev)
    within = column % (2 * order_dev)
    component = within // order_dev
    order = owner * order_dev + within % order_dev
    return (component, order)


def phases(first, second, lon_total):
    phase_index = first[:, None] * second[None, :] % lon_total
    return phase_index.astype(jnp.float32) * (2.0 * math.pi / lon_total)


def per_device(height, east, north, depth, equilibrium, mask, sines, legendre, love):
    lat_rows, lon_cols = height.shape
    order_dev = legendre.shape[2]
    sht_count = lax.axis_size("sht")
    ocean_count = lax.axis_size("ocean")
    lon_total = lon_cols * sht_count
    lat_total = lat_rows * ocean_count
    longitude = lax.axis_index("sht") * lon_cols + jnp.arange(lon_cols, dtype=jnp.int32)
    component, order = decode_columns(2 * order_dev * sht_count, order_dev)
    angles = phases(longitude, order, lon_total)
    analysis = jnp.where(component[None, :] == 0, jnp.cos(angles), -jnp.sin(angles)) / lon_total
    order_angles = phases(order, longitude, lon_total)
    doubling = jnp.where(order == 0, 1.0, 2.0).astype(jnp.float32)[:, None]
    synth_table = (
        jnp.where(component[:, None] == 0, jnp.cos(order_angles), -jnp.sin(order_angles)) * doubling
    )
    wet_cells = mask == 1
    east_coef = (COURANT / jnp.sqrt(1.0 - sines * sines))[:, None]
    coriolis = (ROTATION * sines)[:, None]
    level = jnp.where(wet_cells, height, 0.0)
    eastward, northward = (east, north)
    damping = FRICTION / depth
    for step_index in range(STEPS):
        partial_spectra = jnp.dot(
            level, analysis, precision=HIGHEST, preferred_element_type=jnp.float32
        )
        spectra = lax.psum_scatter(partial_spectra, "sht", scatter_dimension=1, tiled=True)
        weighted = spectra.reshape(lat_rows, 2, order_dev) * (2.0 / lat_total)
        partial_coefs = jnp.einsum("jlm,jcm->lcm", legendre, weighted, precision=HIGHEST)
        coefs = lax.psum(partial_coefs, "ocean")
        loaded = coefs * love[:, None, None]
        synth = jnp.einsum("jlm,lcm->jcm", legendre, loaded, precision=HIGHEST)
        flat_synth = synth.reshape(lat_rows, 2 * order_dev)
        potential = (
            level
            - jnp.dot(
                lax.all_gather(flat_synth, "sht", axis=1, tiled=True),
                synth_table,
                precision=HIGHEST,
                preferred_element_type=jnp.float32,
            )
            - equilibrium
        )
        padded = extended(potential, (("ocean", 0), ("sht", 1)), 1)
        grad_east = east_coef * (padded[1:-1, 2:] - padded[1:-1, :-2])
        grad_north = COURANT * (padded[2:, 1:-1] - padded[:-2, 1:-1])
        new_east = jnp.where(
            wet_cells, eastward + coriolis * northward - grad_east - damping * eastward, 0.0
        )
        new_north = jnp.where(
            wet_cells, northward - coriolis * eastward - grad_north - damping * northward, 0.0
        )
        fluxes = extended(
            jnp.stack([depth * new_east, depth * new_north]), (("ocean", 1), ("sht", 2)), 1
        )
        divergence = east_coef * (fluxes[0, 1:-1, 2:] - fluxes[0, 1:-1, :-2]) + COURANT * (
            fluxes[1, 2:, 1:-1] - fluxes[1, :-2, 1:-1]
        )
        level = jnp.where(wet_cells, level - divergence, 0.0)
        eastward, northward = (new_east, new_north)
    return (level, eastward, northward)


def solution(mesh):
    in_specs = (
        P("ocean", "sht"),
        P("ocean", "sht"),
        P("ocean", "sht"),
        P("ocean", "sht"),
        P("ocean", "sht"),
        P("ocean", "sht"),
        P("ocean"),
        P("ocean", None, "sht"),
        P(),
    )
    out_specs = (P("ocean", "sht"), P("ocean", "sht"), P("ocean", "sht"))
    return jax.shard_map(
        per_device, mesh=mesh, in_specs=in_specs, out_specs=out_specs, check_vma=False
    )
```

profile of v0, /device:TPU:0, one launch (start us, length us, event | category | flops | bytes accessed | tf_op | source)
XLA Modules:
  0.0 939.6 jit_solution(12267016155291331650)
XLA Ops:
  8.1 39.6 %fusion.17 = f32[16,2048]{1,0:T(8,128)} fusion(s32[2048]{0:T(1024)S(1)} %fusion.96, s32[1024]{0:T(1024)S(1)} %iota_add_fusion, pred[2048]{0:T(1024)(128)(4,1)S(1)} %fusion.93, pred[16,1024]{1,0:T(8,128)(4,1)S(1)} %broadcast_compare_fusion, f32[16,1024]{1,0:T(8,128)} %param.9), kind=kOutput, calls=%fused_computation.29 | convolution fusion | flops 438321152 | bytes 227328 | tf_op jit(solution)/shard_map/dot_general | solution.py:67
  48.0 33.2 %copy.19 = f32[16,1024,512]{1,0,2:T(8,128)} copy(f32[16,1024,512]{2,1,0:T(8,128)} %param.16) | data formatting | bytes 67108864 | tf_op args[7]
  82.4 22.0 %convolution_bitcast_fusion.2 = f32[1024,2,512]{0,1,2:T(2,128)} fusion(f32[16,2,512]{0,1,2:T(2,128)S(1)} %copy.21, f32[16,1024,512]{1,0,2:T(8,128)} %copy.19), kind=kOutput, calls=%fused_computation.32 | convolution fusion | flops 201326592 | bytes 37814272 | tf_op jit(solution)/shard_map/jlm,jcm->lcm/dot_general | solution.py:72
  104.5 114.3 %all-reduce.4.cloned.1.call-done = f32[1024,2,512]{0,1,2:T(2,128)} async-done(((f32[1024,2,512]{0,1,2:T(2,128)}), f32[1024,2,512]{0,1,2:T(2,128)}) %all-reduce.4.cloned.1.call-update) | async-done | bytes 4194320 | tf_op jit(solution)/shard_map/psum | solution.py:73
  218.8 41.1 %fusion.21 = f32[16,2,512]{0,1,2:T(2,128)S(1)} fusion(f32[16,1024,512]{1,0,2:T(8,128)} %copy.19, f32[1024,2,512]{0,1,2:T(2,128)} %all-reduce.4.cloned.1.call-done, f32[1024]{0:T(1024)S(1)} %copy-done.2), kind=kOutput, calls=%fused_computation.36 | convolution fusion | flops 202375168 | bytes 37818368 | tf_op jit(solution)/shard_map/jlm,lcm->jcm/dot_general | solution.py:75
  260.1 5.3 all_gather.9
  265.5 39.6 %fusion.31 = f32[16,1024]{1,0:T(8,128)S(1)} fusion(f32[16,1024]{1,0:T(8,128)S(1)} %copy-done.6, f32[16,2048]{1,0:T(8,128)S(1)} %all_gather.9, f32[2048]{0:T(1024)S(1)} %compare_select_fusion, s32[1024]{0:T(1024)S(1)} %iota_add_fusion, s32[2048]{0:T(1024)S(1)} %fusion.96, pred[2048]{0:T(1024)(128)(4,1)S(1)} %fusion.93, ...), kind=kOutput, calls=%fused_computation.40 | convolution fusion | flops 438353920 | bytes 366592 | tf_op jit(solution)/shard_map/dot_general | solution.py:79
  305.2 1.3 collective-permute-start.1
  306.5 3.0 collective-permute-start
  311.7 4.5 collective-permute-start.3
  316.3 1.4 collective-permute-done.3
  317.8 1.3 collective-permute-start.5
  319.1 3.0 collective-permute-start.4
  323.0 1.3 collective-permute-start.6
  324.3 4.7 collective-permute-start.7
  329.1 1.3 collective-permute-done.7
  330.5 38.9 %fusion.16 = f32[16,2048]{1,0:T(8,128)} fusion(f32[16,1024]{1,0:T(8,128)S(1)} %fusion.79, s32[2048]{0:T(1024)S(1)} %fusion.96, s32[1024]{0:T(1024)S(1)} %iota_add_fusion, pred[2048]{0:T(1024)(128)(4,1)S(1)} %fusion.93), kind=kOutput, calls=%fused_computation.28 | convolution fusion | flops 438304768 | bytes 210944 | tf_op jit(solution)/shard_map/dot_general | solution.py:67
  369.7 14.8 %reduce-scatter.6.cloned.1.call-done = f32[16,1024]{1,0:T(8,128)} async-done(((f32[16,2048]{1,0:T(8,128)}), f32[16,1024]{1,0:T(8,128)}) %reduce-scatter.6.cloned.1.call-update) | async-done | bytes 65552 | tf_op jit(solution)/shard_map/reduce_scatter | solution.py:70
  385.6 22.0 %convolution_bitcast_fusion.1 = f32[1024,2,512]{0,1,2:T(2,128)} fusion(f32[16,2,512]{0,1,2:T(2,128)S(1)} %copy.22, f32[16,1024,512]{1,0,2:T(8,128)} %copy.19), kind=kOutput, calls=%fused_computation.31 | convolution fusion | flops 201326592 | bytes 37814272 | tf_op jit(solution)/shard_map/jlm,jcm->lcm/dot_general | solution.py:72
  407.6 111.6 %all-reduce.6.cloned.1.call-done = f32[1024,2,512]{0,1,2:T(2,128)} async-done(((f32[1024,2,512]{0,1,2:T(2,128)}), f32[1024,2,512]{0,1,2:T(2,128)}) %all-reduce.6.cloned.1.call-update) | async-done | bytes 4194320 | tf_op jit(solution)/shard_map/psum | solution.py:73
  519.3 41.1 %fusion.24 = f32[16,2,512]{0,1,2:T(2,128)S(1)} fusion(f32[16,1024,512]{1,0,2:T(8,128)} %copy.19, f32[1024,2,512]{0,1,2:T(2,128)} %all-reduce.6.cloned.1.call-done, f32[1024]{0:T(1024)S(1)} %copy-done.2), kind=kOutput, calls=%fused_computation.37 | convolution fusion | flops 202375168 | bytes 37818368 | tf_op jit(solution)/shard_map/jlm,lcm->jcm/dot_general | solution.py:75
  560.6 5.3 all_gather.10
  566.0 39.6 %fusion.33 = f32[16,1024]{1,0:T(8,128)S(1)} fusion(f32[16,1024]{1,0:T(8,128)S(1)} %copy-done.6, f32[16,1024]{1,0:T(8,128)S(1)} %fusion.79, f32[16,2048]{1,0:T(8,128)S(1)} %all_gather.10, f32[2048]{0:T(1024)S(1)} %compare_select_fusion, s32[1024]{0:T(1024)S(1)} %iota_add_fusion, s32[2048]{0:T(1024)S(1)} %fusion.96, pred[2048]{0:T(1024)(128)(4,1)S(1)} %fusion.93), kind=kOutput, calls=%fused_computation.42 | convolution fusion | flops 438337536 | bytes 350208 | tf_op jit(solution)/shard_map/dot_general | solution.py:79
  605.6 1.3 collective-permute-start.9
  606.9 3.0 collective-permute-start.8
  612.1 4.5 collective-permute-start.11
  616.7 1.4 collective-permute-done.11
  618.2 1.3 collective-permute-start.13
  619.5 3.0 collective-permute-start.12
  623.4 1.3 collective-permute-start.14
  624.7 4.7 collective-permute-start.15
  629.5 1.3 collective-permute-done.15
  630.9 38.9 %fusion.15 = f32[16,2048]{1,0:T(8,128)} fusion(f32[16,1024]{1,0:T(8,128)S(1)} %fusion.60, s32[2048]{0:T(1024)S(1)} %fusion.96, s32[1024]{0:T(1024)S(1)} %iota_add_fusion, pred[2048]{0:T(1024)(128)(4,1)S(1)} %fusion.93), kind=kOutput, calls=%fused_computation.27 | convolution fusion | flops 438304768 | bytes 210944 | tf_op jit(solution)/shard_map/dot_general | solution.py:67
  670.1 14.8 %reduce-scatter.8.cloned.1.call-done = f32[16,1024]{1,0:T(8,128)} async-done(((f32[16,2048]{1,0:T(8,128)}), f32[16,1024]{1,0:T(8,128)}) %reduce-scatter.8.cloned.1.call-update) | async-done | bytes 65552 | tf_op jit(solution)/shard_map/reduce_scatter | solution.py:70
  686.0 22.0 %convolution_bitcast_fusion = f32[1024,2,512]{0,1,2:T(2,128)} fusion(f32[16,2,512]{0,1,2:T(2,128)S(1)} %copy.23, f32[16,1024,512]{1,0,2:T(8,128)} %copy.19), kind=kOutput, calls=%fused_computation.30 | convolution fusion | flops 201326592 | bytes 37814272 | tf_op jit(solution)/shard_map/jlm,jcm->lcm/dot_general | solution.py:72
  708.0 111.6 %all-reduce.8.cloned.1.call-done = f32[1024,2,512]{0,1,2:T(2,128)} async-done(((f32[1024,2,512]{0,1,2:T(2,128)}), f32[1024,2,512]{0,1,2:T(2,128)}) %all-reduce.8.cloned.1.call-update) | async-done | bytes 4194320 | tf_op jit(solution)/shard_map/psum | solution.py:73
  819.6 41.1 %fusion.27 = f32[16,2,512]{0,1,2:T(2,128)S(1)} fusion(f32[16,1024,512]{1,0,2:T(8,128)} %copy.19, f32[1024,2,512]{0,1,2:T(2,128)} %all-reduce.8.cloned.1.call-done, f32[1024]{0:T(1024)S(1)} %copy-done.2), kind=kOutput, calls=%fused_computation.38 | convolution fusion | flops 202375168 | bytes 37818368 | tf_op jit(solution)/shard_map/jlm,lcm->jcm/dot_general | solution.py:75
  860.9 5.2 all_gather.11
  866.1 39.6 %fusion.35 = f32[16,1024]{1,0:T(8,128)S(1)} fusion(f32[16,1024]{1,0:T(8,128)S(1)} %copy-done.6, f32[16,1024]{1,0:T(8,128)S(1)} %fusion.60, f32[16,2048]{1,0:T(8,128)S(1)} %all_gather.11, f32[2048]{0:T(1024)S(1)} %compare_select_fusion, s32[1024]{0:T(1024)S(1)} %iota_add_fusion, s32[2048]{0:T(1024)S(1)} %fusion.96, pred[2048]{0:T(1024)(128)(4,1)S(1)} %fusion.93), kind=kOutput, calls=%fused_computation.44 | convolution fusion | flops 438337536 | bytes 350208 | tf_op jit(solution)/shard_map/dot_general | solution.py:79
  905.7 1.3 collective-permute-start.17
  907.0 3.0 collective-permute-start.16
  912.2 4.5 collective-permute-start.19
  916.8 1.4 collective-permute-done.19
  919.0 1.3 collective-permute-start.21
  920.3 3.0 collective-permute-start.20
  924.2 1.3 collective-permute-start.22
  925.5 4.5 collective-permute-start.23
  930.0 1.5 collective-permute-done.23
  (89 shorter events, 17.2 us)
Async XLA Ops:
  7.2 74.0 %reduce-scatter.4.cloned.1.call-start = ((), (), s32[]{:S(2)}) async-start(), calls=%async_computation.3 | async-start | bytes 196608 | tf_op jit(solution)/shard_map/reduce_scatter | solution.py:70
  47.7 171.0 %all-reduce.4.cloned.1.call-start = ((), (), s32[]{:S(2)}) async-start(), calls=%async_computation.4 | async-start | bytes 8388608 | tf_op jit(solution)/shard_map/psum | solution.py:73
  82.4 136.4 %copy-start.2 = (f32[1024]{0:T(1024)S(1)}, f32[1024]{0:T(1024)}, u32[]{:S(2)}) copy-start(f32[1024]{0:T(1024)} %param.17) | copy-start | bytes 12292
  104.4 280.1 %reduce-scatter.6.cloned.1.call-start = ((), (), s32[]{:S(2)}) async-start(), calls=%async_computation.5 | async-start | bytes 196608 | tf_op jit(solution)/shard_map/reduce_scatter | solution.py:70
  104.4 161.0 %copy-start.5 = (f32[16,1024]{1,0:T(8,128)S(1)}, f32[16,1024]{1,0:T(8,128)}, u32[]{:S(2)}) copy-start(f32[16,1024]{1,0:T(8,128)} %param.9) | copy-start | bytes 196612
  104.4 161.0 %copy-start.6 = (f32[16,1024]{1,0:T(8,128)S(1)}, f32[16,1024]{1,0:T(8,128)}, u32[]{:S(2)}) copy-start(f32[16,1024]{1,0:T(8,128)} %param.13) | copy-start | bytes 196612
  265.5 44.1 %copy-start.7 = (f32[16]{0:T(128)S(1)}, f32[16]{0:T(128)}, u32[]{:S(2)}) copy-start(f32[16]{0:T(128)} %param.15) | copy-start | bytes 196
  265.5 52.2 %copy-start = (s32[16,1024]{1,0:T(8,128)S(1)}, s32[16,1024]{1,0:T(8,128)}, u32[]{:S(2)}) copy-start(s32[16,1024]{1,0:T(8,128)} %param.14) | copy-start | bytes 196612
  265.5 52.2 %copy-start.1 = (f32[16,1024]{1,0:T(8,128)S(1)}, f32[16,1024]{1,0:T(8,128)}, u32[]{:S(2)}) copy-start(f32[16,1024]{1,0:T(8,128)} %param.12) | copy-start | bytes 196612
  265.5 52.1 %copy-start.3 = (f32[16,1024]{1,0:T(8,128)S(1)}, f32[16,1024]{1,0:T(8,128)}, u32[]{:S(2)}) copy-start(f32[16,1024]{1,0:T(8,128)} %param.10) | copy-start | bytes 196612
  265.5 52.1 %copy-start.4 = (f32[16,1024]{1,0:T(8,128)S(1)}, f32[16,1024]{1,0:T(8,128)}, u32[]{:S(2)}) copy-start(f32[16,1024]{1,0:T(8,128)} %param.11) | copy-start | bytes 196612
  305.2 4.4 collective-permute-start.1
  306.5 3.8 collective-permute-start
  310.4 5.8 collective-permute-start.2
  311.7 5.9 collective-permute-start.3
  317.8 4.3 collective-permute-start.5
  319.1 3.8 collective-permute-start.4
  323.0 6.0 collective-permute-start.6
  324.3 6.1 collective-permute-start.7
  369.4 149.9 %all-reduce.6.cloned.1.call-start = ((), (), s32[]{:S(2)}) async-start(), calls=%async_computation.6 | async-start | bytes 8388608 | tf_op jit(solution)/shard_map/psum | solution.py:73
  407.6 277.3 %reduce-scatter.8.cloned.1.call-start = ((), (), s32[]{:S(2)}) async-start(), calls=%async_computation.7 | async-start | bytes 196608 | tf_op jit(solution)/shard_map/reduce_scatter | solution.py:70
  605.6 4.3 collective-permute-start.9
  606.9 3.8 collective-permute-start.8
  610.8 5.8 collective-permute-start.10
  612.1 5.9 collective-permute-start.11
  618.2 4.3 collective-permute-start.13
  619.5 3.8 collective-permute-start.12
  623.4 6.0 collective-permute-start.14
  624.7 6.1 collective-permute-start.15
  669.8 149.8 %all-reduce.8.cloned.1.call-start = ((), (), s32[]{:S(2)}) async-start(), calls=%async_computation.8 | async-start | bytes 8388608 | tf_op jit(solution)/shard_map/psum | solution.py:73
  905.7 4.3 collective-permute-start.17
  907.0 3.8 collective-permute-start.16
  910.9 5.8 collective-permute-start.18
  912.2 5.9 collective-permute-start.19
  919.0 4.3 collective-permute-start.21
  920.3 3.8 collective-permute-start.20
  924.2 5.8 collective-permute-start.22
  925.5 6.1 collective-permute-start.23
Sparse Core Ops, SparseCore 0:
  47.9 12.9 reduce-scatter.3
  104.5 114.2 all-reduce.3
  369.5 14.8 reduce-scatter.5
  407.7 111.5 all-reduce.5
  669.9 14.8 reduce-scatter.7
  708.1 111.4 all-reduce.7
where the time goes:
time: 953 us; the launch traced here: 940 us
  matrix products  425 us (45%)
  waiting for transfers between devices  380 us (40%)
  starting transfers between devices  62.1 us (7%)
  local copies, waits for them, and re-layouts  34.8 us (4%)
  blocking collectives  15.9 us (2%)
  between operations  15.1 us (2%)
    psum x3, waiting for transfers between devices, per_device(): coefs = lax.psum(partial_coefs, 'ocean')  338 us
    dot_general x3, matrix products, per_device(): synth = jnp.einsum('jlm,lcm->jcm', legendre, loaded, precision=HIGHEST)  123 us
    dot_general x3, matrix products, per_device(): jnp.dot(lax.all_gather(flat_synth, 'sht', axis=1, tiled=True), synth_tabl...  119 us
    dot_general x3, matrix products, per_device(): jnp.dot(level, analysis, precision=HIGHEST, preferred_element_type=jnp.fl...  117 us
    dot_general x3, matrix products, per_device(): jnp.einsum('jlm,jcm->lcm', legendre, weighted, precision=HIGHEST)  65.9 us
    ppermute x12, starting transfers between devices, extended(): before = lax.ppermute(last, axis, up)  45.8 us
    unnamed x20, local copies, waits for them, and re-layouts  33.3 us
    reduce_scatter x3, waiting for transfers between devices, per_device(): lax.psum_scatter(partial_spectra, 'sht', scatter_dimension=1, tiled=True)  29.6 us
  transfers between devices with their start and end apart: 30, of which 17 were waited for; matrix products, arithmetic and copies ran while one was open for 4% of the time, Pallas kernels for 0%

commit v1 on v0

v1 whole, which is shorter than its diff:
```python
import functools
import math

import jax
import jax.numpy as jnp
import ml_dtypes
import numpy as np
from jax import lax
from jax.experimental import pallas as pl
from jax.experimental.pallas import tpu as pltpu
from jax.sharding import PartitionSpec as P

STEPS = 3
COURANT = 0.12
ROTATION = 0.5
FRICTION = 0.3
LANES = 128


def fourier_tables(lon_total, order_dev, sht_count):
    k = np.arange(lon_total // 2)[:, None]
    high, low = [], []
    for owner in range(sht_count):
        m = owner * order_dev + np.arange(order_dev)[None, :]
        angle = 2.0 * math.pi * ((k * m) % lon_total) / lon_total
        table = np.concatenate([np.cos(angle), -np.sin(angle)], 1).astype(np.float32)
        top = table.astype(ml_dtypes.bfloat16)
        high.append(top)
        low.append((table - top.astype(np.float32)).astype(ml_dtypes.bfloat16))
    return np.stack(high), np.stack(low)


def split(x):
    top = x.astype(jnp.bfloat16)
    return top, (x - top.astype(jnp.float32)).astype(jnp.bfloat16)


def table_dot(x, high, low, dims):
    rows = x.shape[0]
    top, rest = split(x)
    stacked = jnp.concatenate([top, rest], 0)
    dot = functools.partial(
        lax.dot_general, dimension_numbers=(dims, ((), ())), preferred_element_type=jnp.float32
    )
    main = dot(stacked, high)
    return main[:rows] + main[rows:] + dot(top, low)


def kernel(
    geo,
    height, east, north, depth, equilibrium, mask, sines, love, legendre, table_high, table_low,
    level_out, east_out, north_out,
    leg, high, low, weights, acc, synth,
    pair_send, pair_recv, ring_sum, ring_recv, coefs,
    rows_z, part_out, part_in, pot, flux_e, flux_n,
    halo_top, halo_bottom, halo_left, halo_right,
    load_sem, pair_s, pair_r, ring_s, ring_r, gath_s, gath_r, fwd_s, fwd_r,
    z_s, z_r, sal_s, sal_r, halo_s, halo_r,
):
    rows, cols, order_dev, degrees, sht, ocean = geo
    blocks = order_dev // LANES
    n = ocean // 2
    starts = [0]
    for b in range(blocks):
        starts.append(starts[-1] + degrees - LANES * b)
    chunk = starts[-1] // n
    piece = math.gcd(chunk, LANES)
    pieces = chunk // piece
    lon_total = cols * sht
    lat_total = rows * ocean
    scale = 2.0 / lat_total / lon_total

    o = lax.axis_index("ocean")
    d = lax.axis_index("sht")
    core = lax.rem(o, 2)
    chip = lax.div(o, 2)
    zz, yy = lax.div(chip, 2), lax.rem(chip, 2)
    p = zz * (1 - yy) + (n - 1 - zz) * yy
    back = lax.rem(n - p, n)
    q = p * (1 - core) + back * core
    q_peer = p * core + back * (1 - core)

    def ocean_of(pos):
        far = lax.div(pos, n // 2)
        return 2 * ((1 - far) * 2 * pos + far * (2 * (n - 1 - pos) + 1)) + core

    succ = ocean_of(lax.rem(p + 1 - 2 * core + n, n))
    pred = ocean_of(lax.rem(p - 1 + 2 * core + n, n))
    mate = o + 1 - 2 * core
    below = lax.rem(o + 1, ocean)
    above = lax.rem(o + ocean - 1, ocean)
    right = lax.rem(d + 1, sht)
    left = lax.rem(d + sht - 1, sht)

    loads = []
    for b in range(blocks):
        loads.append(
            pltpu.make_async_copy(
                legendre.at[:, pl.ds(LANES * b, degrees - LANES * b), pl.ds(LANES * b, LANES)],
                leg.at[:, pl.ds(starts[b], degrees - LANES * b), :],
                load_sem.at[b],
            )
        )
    tables = [
        pltpu.make_async_copy(table_high.at[d], high, load_sem.at[blocks]),
        pltpu.make_async_copy(table_low.at[d], low, load_sem.at[blocks + 1]),
    ]
    for copy in tables + loads:
        copy.start()

    barrier = pltpu.get_barrier_semaphore()
    greeted = [{"ocean": i, "sht": d} for i in (succ, pred, mate, below, above)]
    greeted += [{"ocean": o, "sht": lax.rem(d + i, sht)} for i in range(1, sht)]
    for device in greeted:
        pl.semaphore_signal(barrier, inc=1, device_id=device, device_id_type=pl.DeviceIdType.MESH)
    pl.semaphore_wait(barrier, len(greeted))

    def remote(src, dst, send, recv, ocean_to, sht_to):
        return pltpu.make_async_remote_copy(
            src_ref=src,
            dst_ref=dst,
            send_sem=send,
            recv_sem=recv,
            device_id={"ocean": ocean_to, "sht": sht_to},
            device_id_type=pl.DeviceIdType.MESH,
        )

    def ring_copy(s):
        return remote(ring_sum.at[s], ring_recv.at[s], ring_s.at[s], ring_r.at[s], succ, d)

    def pair_copy(s):
        return remote(pair_send.at[s], pair_recv.at[s], pair_s.at[s], pair_r.at[s], mate, d)

    def gather_copy(s):
        at = coefs.at[core, lax.rem(q + 1 - s + n, n)]
        return remote(at, at, gath_s.at[s], gath_r.at[s], succ, d)

    def forward_copy(s):
        at = coefs.at[core, lax.rem(q + 1 - s + n, n)]
        return remote(at, at, fwd_s.at[s], fwd_r.at[s], mate, d)

    def block_of(row):
        b = 0
        for at in starts[1:-1]:
            b = b + (row >= at).astype(jnp.int32)
        return b

    def analyse(c, which, dst):
        @pl.loop(0, pieces)
        def _(i):
            row = which * chunk + i * piece
            b = block_of(row)
            w = [weights[c, b, j] for j in range(rows)]
            for tile in range(piece // 8):
                at = pl.ds(pl.multiple_of(row + tile * 8, 8), 8)
                terms = [leg[j, at, :] * w[j] for j in range(rows)]
                while len(terms) > 1:
                    terms = [x + y for x, y in zip(terms[::2], terms[1::2])]
                dst[pl.ds(pl.multiple_of(i * piece + tile * 8, 8), 8), :] = terms[0]

    def synthesise(c, which):
        @pl.loop(0, pieces)
        def _(i):
            row = which * chunk + i * piece
            b = block_of(row)
            sums = [acc[c, b, j] for j in range(rows)]
            for tile in range(piece // 8):
                at = pl.ds(pl.multiple_of(row + tile * 8, 8), 8)
                x = coefs[c, which, pl.ds(pl.multiple_of(i * piece + tile * 8, 8), 8), :]
                sums = [sums[j] + leg[j, at, :] * x for j in range(rows)]
            for j in range(rows):
                acc[c, b, j] = sums[j]

    lane = lax.broadcasted_iota(jnp.int32, (rows, cols), 1)
    row_id = lax.broadcasted_iota(jnp.int32, (rows, cols), 0)
    order_lane = lax.rem(lax.broadcasted_iota(jnp.int32, (rows, 2 * order_dev), 1), order_dev)
    even = lax.rem(order_lane, 2) == 0
    doubling = jnp.where(order_lane + d * order_dev == 0, 1.0, 2.0)

    def shifted(x, axis, forward, edge):
        size = x.shape[axis]
        place = (row_id, lane)[axis]
        if forward:
            return jnp.where(place == size - 1, edge, pltpu.roll(x, size - 1, axis))
        return jnp.where(place == 0, edge, pltpu.roll(x, 1, axis))

    sine = sines[...]
    east_coef = COURANT / jnp.sqrt(1.0 - sine * sine)
    coriolis = ROTATION * sine

    level_out[...] = jnp.where(mask[...] == 1, height[...], 0.0)
    east_out[...] = east[...]
    north_out[...] = north[...]
    for copy in tables:
        copy.wait()

    @pl.loop(0, STEPS)
    def _(step):
        rows_z[d] = level_out[...]
        z_copies = [
            remote(rows_z.at[d], rows_z.at[d], z_s.at[i], z_r.at[i], o, lax.rem(d + i, sht))
            for i in range(1, sht)
        ]
        for copy in z_copies:
            copy.start()
        for copy in z_copies:
            copy.wait()
        first = [rows_z[i] for i in range(sht // 2)]
        second = [rows_z[i + sht // 2] for i in range(sht // 2)]
        plus = jnp.concatenate([x + y for x, y in zip(first, second)], 1)
        minus = jnp.concatenate([x - y for x, y in zip(first, second)], 1)
        sums = table_dot(
            jnp.concatenate([plus, minus], 0), high[...], low[...], (((1,), (0,)))
        )
        spectra = jnp.where(even, sums[:rows], sums[rows:]) * scale
        for c in range(2):
            for b in range(blocks):
                at = c * order_dev + b * LANES
                for j in range(rows):
                    weights[c, b, j] = jnp.broadcast_to(
                        spectra[j : j + 1, at : at + LANES], (8, LANES)
                    )
        acc[...] = jnp.zeros_like(acc)

        @pl.when(step == 0)
        def _():
            for copy in loads:
                copy.wait()

        @pl.loop(0, n)
        def _(s):
            analyse(1 - core, lax.rem(q_peer - s + n, n), pair_send.at[s])
            pair_copy(s).start()
            analyse(core, lax.rem(q - s + n, n), ring_sum.at[s])
            pair_copy(s).wait_recv()
            ring_sum[s] = ring_sum[s] + pair_recv[s]

            @pl.when(s > 0)
            def _():
                ring_copy(s - 1).wait_recv()
                ring_sum[s] = ring_sum[s] + ring_recv[s - 1]

            @pl.when(s < n - 1)
            def _():
                ring_copy(s).start()

        coefs[core, lax.rem(q + 1, n)] = ring_sum[n - 1] * love[...]

        @pl.loop(0, n)
        def _(s):
            @pl.when(s > 0)
            def _():
                gather_copy(s - 1).wait_recv()

            @pl.when(s < n - 1)
            def _():
                gather_copy(s).start()

            forward_copy(s).start()
            synthesise(core, lax.rem(q + 1 - s + n, n))
            forward_copy(s).wait_recv()
            synthesise(1 - core, lax.rem(q_peer + 1 - s + n, n))

        @pl.loop(0, n)
        def _(s):
            pair_copy(s).wait_send()
            forward_copy(s).wait_send()

            @pl.when(s < n - 1)
            def _():
                ring_copy(s).wait_send()
                gather_copy(s).wait_send()

        for c in range(2):
            for b in range(blocks):
                at = c * order_dev + b * LANES
                synth[:, at : at + LANES] = jnp.sum(acc[c, b], axis=1)
        y = synth[...] * doubling
        halves = table_dot(
            jnp.concatenate([jnp.where(even, y, 0.0), jnp.where(even, 0.0, y)], 0),
            high[...], low[...], (((1,), (1,))),
        )
        both = (halves[:rows] + halves[rows:], halves[:rows] - halves[rows:])
        for i in range(sht):
            at = (i % (sht // 2)) * cols
            part_out[i] = both[i // (sht // 2)][:, at : at + cols]
        part_in[d] = part_out[d]
        sal_copies = []
        for i in range(1, sht):
            to = lax.rem(d + i, sht)
            sal_copies.append(
                remote(part_out.at[to], part_in.at[d], sal_s.at[i], sal_r.at[i], o, to)
            )
        for copy in sal_copies:
            copy.start()
        for copy in sal_copies:
            copy.wait()
        sal = part_in[0]
        for i in range(1, sht):
            sal = sal + part_in[i]

        wet = mask[...] == 1
        pot[...] = level_out[...] - sal - equilibrium[...]
        copies = [
            remote(pot.at[pl.ds(rows - 8, 8)], halo_top.at[0], halo_s.at[0], halo_r.at[0], below, d),
            remote(pot.at[pl.ds(0, 8)], halo_bottom.at[0], halo_s.at[1], halo_r.at[1], above, d),
            remote(
                pot.at[:, pl.ds(cols - LANES, LANES)], halo_left.at[0],
                halo_s.at[2], halo_r.at[2], o, right,
            ),
            remote(
                pot.at[:, pl.ds(0, LANES)], halo_right.at[0],
                halo_s.at[3], halo_r.at[3], o, left,
            ),
        ]
        for copy in copies:
            copy.start()
        for copy in copies:
            copy.wait()
        here = pot[...]
        grad_east = east_coef * (
            shifted(here, 1, True, halo_right[0][:, :1])
            - shifted(here, 1, False, halo_left[0][:, LANES - 1 :])
        )
        grad_north = COURANT * (
            shifted(here, 0, True, halo_bottom[0][:1, :])
            - shifted(here, 0, False, halo_top[0][7:, :])
        )
        old_east, old_north = east_out[...], north_out[...]
        deep = depth[...]
        damping = FRICTION / deep
        new_east = jnp.where(
            wet, old_east + coriolis * old_north - grad_east - damping * old_east, 0.0
        )
        new_north = jnp.where(
            wet, old_north - coriolis * old_east - grad_north - damping * old_north, 0.0
        )
        east_out[...] = new_east
        north_out[...] = new_north
        flux_e[...] = deep * new_east
        flux_n[...] = deep * new_north
        copies = [
            remote(
                flux_n.at[pl.ds(rows - 8, 8)], halo_top.at[1], halo_s.at[4], halo_r.at[4], below, d
            ),
            remote(flux_n.at[pl.ds(0, 8)], halo_bottom.at[1], halo_s.at[5], halo_r.at[5], above, d),
            remote(
                flux_e.at[:, pl.ds(cols - LANES, LANES)], halo_left.at[1],
                halo_s.at[6], halo_r.at[6], o, right,
            ),
            remote(
                flux_e.at[:, pl.ds(0, LANES)], halo_right.at[1],
                halo_s.at[7], halo_r.at[7], o, left,
            ),
        ]
        for copy in copies:
            copy.start()
        for copy in copies:
            copy.wait()
        fe, fn = flux_e[...], flux_n[...]
        divergence = east_coef * (
            shifted(fe, 1, True, halo_right[1][:, :1])
            - shifted(fe, 1, False, halo_left[1][:, LANES - 1 :])
        ) + COURANT * (
            shifted(fn, 0, True, halo_bottom[1][:1, :])
            - shifted(fn, 0, False, halo_top[1][7:, :])
        )
        level_out[...] = jnp.where(wet, level_out[...] - divergence, 0.0)


def per_device(height, east, north, depth, equilibrium, mask, sines, legendre, love):
    rows, cols = height.shape
    degrees, order_dev = legendre.shape[1:]
    sht = lax.axis_size("sht")
    ocean = lax.axis_size("ocean")
    blocks = order_dev // LANES
    n = ocean // 2
    packed = sum(degrees - LANES * b for b in range(blocks))
    chunk = packed // n
    high, low = fourier_tables(cols * sht, order_dev, sht)

    o = lax.axis_index("ocean")
    core, chip = o % 2, o // 2
    p = jnp.where(chip % 2 == 0, chip // 2, n - 1 - chip // 2)
    q = jnp.where(core == 0, p, (n - p) % n)
    packed_love = jnp.concatenate([love[LANES * b :] for b in range(blocks)])
    own_love = lax.dynamic_slice(packed_love, (((q + 1) % n) * chunk,), (chunk,))
    own_love = jnp.broadcast_to(own_love[:, None], (chunk, LANES))

    f32 = jnp.float32
    vmem = pl.BlockSpec(memory_space=pltpu.VMEM)
    hbm = pl.BlockSpec(memory_space=pl.ANY)
    dma = lambda k: pltpu.SemaphoreType.DMA((k,))
    half = cols * sht // 2
    grid = jax.ShapeDtypeStruct((rows, cols), f32)
    return pl.pallas_call(
        functools.partial(kernel, (rows, cols, order_dev, degrees, sht, ocean)),
        out_shape=(grid, grid, grid),
        in_specs=[vmem] * 8 + [hbm] * 3,
        out_specs=(vmem, vmem, vmem),
        scratch_shapes=[
            pltpu.VMEM((rows, packed, LANES), f32),
            pltpu.VMEM((half, 2 * order_dev), jnp.bfloat16),
            pltpu.VMEM((half, 2 * order_dev), jnp.bfloat16),
            pltpu.VMEM((2, blocks, rows, 8, LANES), f32),
            pltpu.VMEM((2, blocks, rows, 8, LANES), f32),
            pltpu.VMEM((rows, 2 * order_dev), f32),
            pltpu.VMEM((n, chunk, LANES), f32),
            pltpu.VMEM((n, chunk, LANES), f32),
            pltpu.VMEM((n, chunk, LANES), f32),
            pltpu.VMEM((n, chunk, LANES), f32),
            pltpu.VMEM((2, n, chunk, LANES), f32),
            pltpu.VMEM((sht, rows, cols), f32),
            pltpu.VMEM((sht, rows, cols), f32),
            pltpu.VMEM((sht, rows, cols), f32),
            pltpu.VMEM((rows, cols), f32),
            pltpu.VMEM((rows, cols), f32),
            pltpu.VMEM((rows, cols), f32),
            pltpu.VMEM((2, 8, cols), f32),
            pltpu.VMEM((2, 8, cols), f32),
            pltpu.VMEM((2, rows, LANES), f32),
            pltpu.VMEM((2, rows, LANES), f32),
            dma(blocks + 2),
            dma(n), dma(n), dma(n), dma(n), dma(n), dma(n), dma(n), dma(n),
            dma(sht), dma(sht), dma(sht), dma(sht), dma(8), dma(8),
        ],
        compiler_params=pltpu.CompilerParams(
            collective_id=0, has_side_effects=True, vmem_limit_bytes=60 * 1024 * 1024
        ),
    )(
        height, east, north, depth, equilibrium, mask, sines[:, None], own_love, legendre,
        jnp.asarray(high), jnp.asarray(low),
    )


def solution(mesh):
    grid = P("ocean", "sht")
    in_specs = (grid,) * 6 + (P("ocean"), P("ocean", None, "sht"), P())
    return jax.shard_map(
        per_device, mesh=mesh, in_specs=in_specs, out_specs=(grid,) * 3, check_vma=False
    )
```

time: 953 us -> 281 us (0.29); the launches traced: 940 us -> 281 us
  matrix products: 425 us -> 0 us
  waiting for transfers between devices: 380 us -> 0 us
  Pallas kernels: 0 us -> 271 us
  starting transfers between devices: 62.1 us -> 0 us
  local copies, waits for them, and re-layouts: 34.8 us -> 8.62 us
  blocking collectives: 15.9 us -> 0 us
  between operations: 15.1 us -> 0.73 us
    dot_general x12 -> x0, matrix products: 425 us -> none  [the longest x3 123 us: per_device(): synth = jnp.einsum('jlm,lcm->jcm', legendre, loaded, precision=HIGHEST)]
    psum x3 -> x0, waiting for transfers between devices: 338 us -> none  [per_device(): coefs = lax.psum(partial_coefs, 'ocean')]
    pallas_call x0 -> x1, Pallas kernels: none -> 271 us  [per_device(): pl.pallas_call(functools.partial(kernel, (rows, cols, order_dev, degrees,...]
    ppermute x24 -> x0, starting transfers between devices: 61.2 us -> none  [the longest x12 45.8 us: extended(): before = lax.ppermute(last, axis, up)]
    reduce_scatter x3 -> x0, waiting for transfers between devices: 29.6 us -> none  [per_device(): lax.psum_scatter(partial_spectra, 'sht', scatter_dimension=1, tiled=True)]
    unnamed x20 -> x3, local copies, waits for them, and re-layouts: 33.3 us -> 4.42 us
    all_gather x3 -> x0, blocking collectives: 15.9 us -> none  [per_device(): lax.all_gather(flat_synth, 'sht', axis=1, tiled=True)]
    ppermute x24 -> x0, waiting for transfers between devices: 13.1 us -> none  [the longest x12 13 us: extended(): before = lax.ppermute(last, axis, up)]
  transfers between devices with their start and end apart: 30 -> 0, of which waited for: 17 -> 0; matrix products, arithmetic and copies ran while one was open for 4% -> 0% of each run, Pallas kernels for 0% -> 0%
where the time goes in v1:
time: 281 us
  Pallas kernels  271 us (96%)
  local copies, waits for them, and re-layouts  8.62 us (3%)
    pallas_call x1, Pallas kernels, per_device(): pl.pallas_call(functools.partial(kernel, (rows, cols, order_dev, degrees,...  271 us

profile of v1, /device:TPU:0, one launch (start us, length us, event | category | flops | bytes accessed | tf_op | source)
XLA Modules:
  0.0 280.6 jit_solution(11959682943333585864)
XLA Ops:
  0.7 0.7 slice.10
  1.4 0.7 slice.9
  2.1 0.7 slice.11
  2.8 0.8 fusion.2
  3.6 1.3 copy.14.sines
  4.9 0.8 broadcast_in_dim.10.love
  5.7 270.5 %shard_map.130 = (f32[16,1024]{1,0:T(8,128)}, f32[16,1024]{1,0:T(8,128)}, f32[16,1024]{1,0:T(8,128)}) custom-call(f32[16,1024]{1,0:T(8,128)} %height.1, f32[16,1024]{1,0:T(8,128)} %east.1, f32[16,1024]{1,0:T(8,128)} %north.1, f32[16,1024]{1,0:T(8,128)} %depth.1, f32[16,1024]{1,0:T(8,128)} %equilibrium.1, s32[16,1024]{1,0:T(8,128)} %mask.1, ...), custom_call_target="tpu_custom_call" | custom-call | tf_op jit(solution)/shard_map/pallas_call | solution.py:396
  276.2 1.5 copy.18
  277.7 1.5 copy.19
  279.2 1.5 copy.20

commit v2 on v1

--- a/solution.py
+++ b/solution.py
@@ -64,8 +64,10 @@
     for b in range(blocks):
         starts.append(starts[-1] + degrees - LANES * b)
     chunk = starts[-1] // n
-    piece = math.gcd(chunk, LANES)
+    piece = math.gcd(chunk, 32)
     pieces = chunk // piece
+    cut = (pieces + 1) // 2
+    spans = ((0, cut), (cut, pieces))
     lon_total = cols * sht
     lat_total = rows * ocean
     scale = 2.0 / lat_total / lon_total
@@ -125,19 +127,24 @@
             device_id_type=pl.DeviceIdType.MESH,
         )
 
-    def ring_copy(s):
-        return remote(ring_sum.at[s], ring_recv.at[s], ring_s.at[s], ring_r.at[s], succ, d)
-
-    def pair_copy(s):
-        return remote(pair_send.at[s], pair_recv.at[s], pair_s.at[s], pair_r.at[s], mate, d)
-
-    def gather_copy(s):
-        at = coefs.at[core, lax.rem(q + 1 - s + n, n)]
-        return remote(at, at, gath_s.at[s], gath_r.at[s], succ, d)
-
-    def forward_copy(s):
-        at = coefs.at[core, lax.rem(q + 1 - s + n, n)]
-        return remote(at, at, fwd_s.at[s], fwd_r.at[s], mate, d)
+    def part(h):
+        return pl.ds(spans[h][0] * piece, (spans[h][1] - spans[h][0]) * piece)
+
+    def ring_copy(s, h):
+        src, dst = ring_sum.at[s, part(h), :], ring_recv.at[s, part(h), :]
+        return remote(src, dst, ring_s.at[h, s], ring_r.at[h, s], succ, d)
+
+    def pair_copy(s, h):
+        src, dst = pair_send.at[s, part(h), :], pair_recv.at[s, part(h), :]
+        return remote(src, dst, pair_s.at[h, s], pair_r.at[h, s], mate, d)
+
+    def gather_copy(s, h):
+        at = coefs.at[core, lax.rem(q + 1 - s + n, n), part(h), :]
+        return remote(at, at, gath_s.at[h, s], gath_r.at[h, s], succ, d)
+
+    def forward_copy(s, h):
+        at = coefs.at[core, lax.rem(q + 1 - s + n, n), part(h), :]
+        return remote(at, at, fwd_s.at[h, s], fwd_r.at[h, s], mate, d)
 
     def block_of(row):
         b = 0
@@ -145,8 +152,8 @@
             b = b + (row >= at).astype(jnp.int32)
         return b
 
-    def analyse(c, which, dst):
-        @pl.loop(0, pieces)
+    def analyse(c, which, dst, h):
+        @pl.loop(*spans[h])
         def _(i):
             row = which * chunk + i * piece
             b = block_of(row)
@@ -158,8 +165,8 @@
                     terms = [x + y for x, y in zip(terms[::2], terms[1::2])]
                 dst[pl.ds(pl.multiple_of(i * piece + tile * 8, 8), 8), :] = terms[0]
 
-    def synthesise(c, which):
-        @pl.loop(0, pieces)
+    def synthesise(c, which, h):
+        @pl.loop(*spans[h])
         def _(i):
             row = which * chunk + i * piece
             b = block_of(row)
@@ -229,47 +236,53 @@
 
         @pl.loop(0, n)
         def _(s):
-            analyse(1 - core, lax.rem(q_peer - s + n, n), pair_send.at[s])
-            pair_copy(s).start()
-            analyse(core, lax.rem(q - s + n, n), ring_sum.at[s])
-            pair_copy(s).wait_recv()
-            ring_sum[s] = ring_sum[s] + pair_recv[s]
-
-            @pl.when(s > 0)
-            def _():
-                ring_copy(s - 1).wait_recv()
-                ring_sum[s] = ring_sum[s] + ring_recv[s - 1]
-
-            @pl.when(s < n - 1)
-            def _():
-                ring_copy(s).start()
+            for h in range(2):
+                analyse(1 - core, lax.rem(q_peer - s + n, n), pair_send.at[s], h)
+                pair_copy(s, h).start()
+                analyse(core, lax.rem(q - s + n, n), ring_sum.at[s], h)
+                pair_copy(s, h).wait_recv()
+                ring_sum[s, part(h), :] = ring_sum[s, part(h), :] + pair_recv[s, part(h), :]
+
+                @pl.when(s > 0)
+                def _():
+                    ring_copy(s - 1, h).wait_recv()
+                    ring_sum[s, part(h), :] = (
+                        ring_sum[s, part(h), :] + ring_recv[s - 1, part(h), :]
+                    )
+
+                @pl.when(s < n - 1)
+                def _():
+                    ring_copy(s, h).start()
 
         coefs[core, lax.rem(q + 1, n)] = ring_sum[n - 1] * love[...]
 
         @pl.loop(0, n)
         def _(s):
-            @pl.when(s > 0)
-            def _():
-                gather_copy(s - 1).wait_recv()
-
-            @pl.when(s < n - 1)
-            def _():
-                gather_copy(s).start()
-
-            forward_copy(s).start()
-            synthesise(core, lax.rem(q + 1 - s + n, n))
-            forward_copy(s).wait_recv()
-            synthesise(1 - core, lax.rem(q_peer + 1 - s + n, n))
+            for h in range(2):
+
+                @pl.when(s > 0)
+                def _():
+                    gather_copy(s - 1, h).wait_recv()
+
+                @pl.when(s < n - 1)
+                def _():
+                    gather_copy(s, h).start()
+
+                forward_copy(s, h).start()
+                synthesise(core, lax.rem(q + 1 - s + n, n), h)
+                forward_copy(s, h).wait_recv()
+                synthesise(1 - core, lax.rem(q_peer + 1 - s + n, n), h)
 
         @pl.loop(0, n)
         def _(s):
-            pair_copy(s).wait_send()
-            forward_copy(s).wait_send()
-
-            @pl.when(s < n - 1)
-            def _():
-                ring_copy(s).wait_send()
-                gather_copy(s).wait_send()
+            for h in range(2):
+                pair_copy(s, h).wait_send()
+                forward_copy(s, h).wait_send()
+
+                @pl.when(s < n - 1)
+                def _():
+                    ring_copy(s, h).wait_send()
+                    gather_copy(s, h).wait_send()
 
         for c in range(2):
             for b in range(blocks):
@@ -421,7 +434,7 @@
             pltpu.VMEM((2, rows, LANES), f32),
             pltpu.VMEM((2, rows, LANES), f32),
             dma(blocks + 2),
-            dma(n), dma(n), dma(n), dma(n), dma(n), dma(n), dma(n), dma(n),
+            *[pltpu.SemaphoreType.DMA((2, n))] * 8,
             dma(sht), dma(sht), dma(sht), dma(sht), dma(8), dma(8),
         ],
         compiler_params=pltpu.CompilerParams(

time: 281 us -> 242 us (0.86)
  Pallas kernels: 271 us -> 231 us
    pallas_call x1, Pallas kernels: 271 us -> 231 us  [per_device(): pl.pallas_call(functools.partial(kernel, (rows, cols, order_dev, degrees,...]
where the time goes in v2:
time: 242 us; the launch traced here: 241 us
  Pallas kernels  231 us (95%)
  local copies, waits for them, and re-layouts  8.62 us (4%)
    pallas_call x1, Pallas kernels, per_device(): pl.pallas_call(functools.partial(kernel, (rows, cols, order_dev, degrees,...  231 us

profile of v2, /device:TPU:0, one launch (start us, length us, event | category | flops | bytes accessed | tf_op | source)
XLA Modules:
  0.0 241.5 jit_solution(10439528476080749338)
XLA Ops:
  0.7 0.7 slice.10
  1.4 0.7 slice.9
  2.1 0.7 slice.11
  2.8 0.8 fusion.2
  3.6 1.3 copy.14.sines
  4.9 0.8 broadcast_in_dim.10.love
  5.7 231.4 %shard_map.130 = (f32[16,1024]{1,0:T(8,128)}, f32[16,1024]{1,0:T(8,128)}, f32[16,1024]{1,0:T(8,128)}) custom-call(f32[16,1024]{1,0:T(8,128)} %height.1, f32[16,1024]{1,0:T(8,128)} %east.1, f32[16,1024]{1,0:T(8,128)} %north.1, f32[16,1024]{1,0:T(8,128)} %depth.1, f32[16,1024]{1,0:T(8,128)} %equilibrium.1, s32[16,1024]{1,0:T(8,128)} %mask.1, ...), custom_call_target="tpu_custom_call" | custom-call | tf_op jit(solution)/shard_map/pallas_call | solution.py:409
  237.1 1.5 copy.18
  238.5 1.5 copy.19
  240.0 1.5 copy.20
